TPU v7x, 32 devices: a whole 2x2x4 slice. The times are simulated.
32 devices in a mesh: member: 2 (over x), gx: 16 (over z, y, core).
Axes of the slice: x: 2, y: 2, z: 4, core: 2. Of those that a mesh axis runs over, the one named last changes fastest.
Arguments:
- fields: bfloat16 [5, 32, 64, 512], P(None, ('member', 'gx')), parts along dimension 1, may hold values from -6 to 6
- adjoint_seed: bfloat16 [5, 32, 64, 512], P(None, ('member', 'gx')), parts along dimension 1, may hold values from -6 to 6
- velocity: bfloat16 [3, 32, 64, 512], P(None, ('member', 'gx')), parts along dimension 1, may hold values from -6 to 6
- activity: int32 [32, 64], P(('member', 'gx')), parts along dimension 0, may hold values from 0 to 1, as said below
- diffusivity: float32 [5], replicated, may hold values from 0.05 to 0.5
- gram_cotangent: float32 [5, 5], replicated, may hold values from -262144 to 262144
Outputs:
- field_gradient: float32 [5, 32, 64, 512], P(None, ('member', 'gx')), parts along dimension 1
There are 2 independent parts, one for each index of `member`. A program takes and returns all parts, laid end to end along the dimension named above; an argument that names none is the same for every part. Nothing has to cross between parts.
Inputs may be any that keep to these rules, and one draw needn't show every extreme that they name: `activity`: each layer holds at most 48 fluid elements and at least one; at least one layer holds exactly 48.
All inputs are finite; a program needn't handle non-finite values.
Results may differ from a plain program's by a relative error of at most 0.0054.
Values sent between devices are 32-bit elements; how exact they have to be, the bound alone decides.
A program may use at most 64 MiB of HBM per device.

v0:
```python
import functools
import jax
import jax.numpy as jnp
import ml_dtypes
import numpy as np
from jax import lax
from jax.experimental import pallas as pl
from jax.experimental.pallas import tpu as pltpu
from jax.sharding import PartitionSpec as P

EY = 4
EZ = 16
F32 = jnp.float32
BF16 = jnp.bfloat16


def basis_tables():
    degree = 7
    gll_points = np.array(
        [
            -1.0,
            -0.8717401485096066,
            -0.5917001814331423,
            -0.2092992179024789,
            0.2092992179024789,
            0.5917001814331423,
            0.8717401485096066,
            1.0,
        ]
    )
    prev_poly = np.ones(8)
    this_poly = gll_points.copy()
    for level in range(1, degree):
        prev_poly, this_poly = (
            this_poly,
            ((2 * level + 1) * gll_points * this_poly - level * prev_poly) / (level + 1),
        )
    gll_weights = 2.0 / (degree * (degree + 1) * this_poly**2)
    deriv = np.zeros((8, 8))
    for row_index in range(8):
        for col_index in range(8):
            if row_index != col_index:
                deriv[row_index, col_index] = this_poly[row_index] / (
                    this_poly[col_index] * (gll_points[row_index] - gll_points[col_index])
                )
    deriv[0, 0] = -degree * (degree + 1) / 4.0
    deriv[7, 7] = degree * (degree + 1) / 4.0
    weight_cube = (
        gll_weights[:, None, None] * gll_weights[None, :, None] * gll_weights[None, None, :]
    ).reshape(512)
    return (weight_cube, deriv)


def constants():
    weight_np, deriv_np = basis_tables()
    dmat = deriv_np.astype(np.float32).astype(ml_dtypes.bfloat16).astype(np.float32)
    lanes = np.arange(512)
    pieces = []
    for index in (lanes // 64, (lanes[:128] // 8) % 8, lanes[:128] % 8):
        pieces += [dmat[:, index], dmat.T[:, index]]
    pieces.append(np.broadcast_to(weight_np.astype(np.float32)[None], (8, 512)))
    return np.ascontiguousarray(np.concatenate(pieces, 1).astype(np.float32))


def build_tables(spread, fa, fbc, ba, bbc, bfa, bfbc):
    row64 = lax.broadcasted_iota(jnp.int32, (64, 512), 0)
    lane64 = lax.broadcasted_iota(jnp.int32, (64, 512), 1) & 63
    same = row64 == lane64
    low = lax.broadcasted_iota(jnp.int32, (64, 128), 1) < 64
    for p in range(8):
        rs = slice(p * 64, p * 64 + 64)
        plain = jnp.where(same, spread[p:p + 1, 0:512], 0.0).astype(BF16)
        ba[rs] = plain
        bfa[rs] = jnp.where(low, plain[:, 0:128], plain[:, 384:512])
        fa[rs] = jnp.where(same, spread[p:p + 1, 512:1024], 0.0).astype(BF16)
    row = lax.broadcasted_iota(jnp.int32, (128, 128), 0)
    lane = lax.broadcasted_iota(jnp.int32, (128, 128), 1)
    b_same = ((row & 7) == (lane & 7)) & ((row >> 6) == (lane >> 6))
    c_same = (row >> 3) == (lane >> 3)

    def b_table(at):
        rows = [jnp.broadcast_to(spread[g % 8:g % 8 + 1, at:at + 128], (8, 128)) for g in range(16)]
        return jnp.where(b_same, jnp.concatenate(rows, 0), 0.0).astype(BF16)

    def c_table(at):
        return jnp.where(c_same, jnp.concatenate([spread[:, at:at + 128]] * 16, 0), 0.0).astype(BF16)

    zero = jnp.zeros((128, 128), BF16)
    b, bt, c, ct = b_table(1024), b_table(1152), c_table(1280), c_table(1408)
    for k, (back, fwd) in enumerate(((b, bt), (c, ct))):
        fbc[0:128, k * 256:k * 256 + 256] = jnp.concatenate([fwd, zero], 1)
        fbc[128:256, k * 256:k * 256 + 256] = jnp.concatenate([zero, fwd], 1)
        bbc[k * 256:k * 256 + 128] = jnp.concatenate([back, zero], 1)
        bbc[k * 256 + 128:k * 256 + 256] = jnp.concatenate([zero, back], 1)
        bfbc[k * 128:k * 128 + 128] = back


def kernel(
    n, nf, ne,
    diff, gram, act, fld_hbm, lam_hbm, vel_hbm, spread_hbm,
    out,
    fld, lam, vel, fa, fbc, ba, bbc, bfa, bfbc, spread,
    lw, q0, qbc, base, mixed, plain,
    part, parts, sbuf, rbuf,
    in_sem, psend, precv, fsend, frecv,
):
    me = lax.axis_index("gx")
    rows = nf * ne
    half = rows // 2

    pairs = ((spread_hbm, spread), (fld_hbm, fld), (lam_hbm, lam), (vel_hbm, vel))
    loads = [pltpu.make_async_copy(s, d, in_sem.at[i]) for i, (s, d) in enumerate(pairs)]
    for load in loads:
        load.start()
    l_spread, l_fld, l_lam, l_vel = loads

    barrier = pltpu.get_barrier_semaphore()

    @pl.loop(1, n)
    def _(o):
        pl.semaphore_signal(barrier, inc=1, device_id={"gx": lax.rem(me + o, n)}, device_id_type=pl.DeviceIdType.MESH)

    @pl.when(me == 0)
    def _():
        rbuf[0] = jnp.zeros((half, 128), F32)
        rbuf[2] = jnp.zeros((half, 128), F32)

    @pl.when(me == n - 1)
    def _():
        rbuf[1] = jnp.zeros((half, 128), F32)
        rbuf[3] = jnp.zeros((half, 128), F32)

    row = lax.broadcasted_iota(jnp.int32, (ne, 128), 0)
    lane = lax.broadcasted_iota(jnp.int32, (ne, 128), 1)
    low = lane < 64
    low_half = lax.broadcasted_iota(jnp.int32, (half, 128), 1) < 64
    c_id, b_id = lane & 7, (lane >> 3) & 7
    j_id, k_id = row >> 4, row & 15
    z_hi = (c_id == 7) & (k_id < EZ - 1)
    z_lo = (c_id == 0) & (k_id > 0)
    y_hi = (b_id == 7) & (j_id < EY - 1)
    y_lo = (b_id == 0) & (j_id > 0)

    def plane_sum(x):
        up, down = pltpu.roll(x, ne - 1, 0), pltpu.roll(x, 1, 0)
        x = x + jnp.where(z_hi, pltpu.roll(up, 7, 1), 0.0) + jnp.where(z_lo, pltpu.roll(down, 121, 1), 0.0)
        up = jnp.concatenate([x[EZ:], x[:EZ]], 0)
        down = jnp.concatenate([x[ne - EZ:], x[: ne - EZ]], 0)
        return x + jnp.where(y_hi, pltpu.roll(up, 56, 1), 0.0) + jnp.where(y_lo, pltpu.roll(down, 72, 1), 0.0)

    flag_row = jnp.broadcast_to(act[...].astype(F32), (ne, ne))
    diag = lax.broadcasted_iota(jnp.int32, (ne, ne), 0) == lax.broadcasted_iota(jnp.int32, (ne, ne), 1)
    mask = jnp.dot(
        jnp.where(diag, flag_row, 0.0).astype(BF16), jnp.ones((ne, 128), BF16), preferred_element_type=F32
    )
    sym = [[(gram[f, h] + gram[h, f]) * 0.5 for h in range(nf)] for f in range(nf)]

    l_spread.wait()
    wts = spread[0:8, 1536:2048]
    build_tables(spread, fa, fbc, ba, bbc, bfa, bfbc)
    l_fld.wait()
    t_acc = jnp.zeros((8, 128), F32)
    b_acc = jnp.zeros((8, 128), F32)
    for ct in range(4):
        cols = slice(ct * 128, ct * 128 + 128)
        u = [fld[f * ne:(f + 1) * ne, cols].astype(F32) for f in range(nf)]
        square = sum(x * x for x in u)
        quad = 0.0
        for f in range(nf):
            inner = sym[f][f] * u[f]
            for h in range(f + 1, nf):
                inner = inner + (2.0 * sym[f][h]) * u[h]
            quad = quad + u[f] * inner
        mw = mask * wts[0:1, cols]
        t_acc = t_acc + jnp.sum((mw * square).reshape(ne // 8, 8, 128), 0)
        b_acc = b_acc + jnp.sum((mw * quad).reshape(ne // 8, 8, 128), 0)
    part[0:8] = t_acc
    part[8:16] = b_acc

    pl.semaphore_wait(barrier, n - 1)

    @pl.loop(1, n)
    def _(o):
        pltpu.make_async_remote_copy(
            src_ref=part, dst_ref=parts.at[o - 1], send_sem=psend.at[o - 1], recv_sem=precv.at[o - 1],
            device_id={"gx": lax.rem(me + o, n)}, device_id_type=pl.DeviceIdType.MESH,
        ).start()

    def face_copy(slot):
        target = me - 1 if slot % 2 == 0 else me + 1
        there = slot + 1 if slot % 2 == 0 else slot - 1
        return pltpu.make_async_remote_copy(
            src_ref=sbuf.at[slot], dst_ref=rbuf.at[there], send_sem=fsend.at[slot], recv_sem=frecv.at[there],
            device_id={"gx": target}, device_id_type=pl.DeviceIdType.MESH,
        )

    def pack(face, slot):
        a, b = face[:half], face[half:]
        sbuf[slot] = jnp.where(low_half, a, pltpu.roll(b, 64, 1))
        sbuf[slot + 1] = jnp.where(low_half, pltpu.roll(a, 64, 1), b)

        @pl.when(me > 0)
        def _():
            face_copy(slot).start()

        @pl.when(me < n - 1)
        def _():
            face_copy(slot + 1).start()

    def unpack(slot):
        p, q = rbuf[slot], rbuf[slot + 1]
        return jnp.concatenate(
            [jnp.where(low_half, p, pltpu.roll(q, 64, 1)), jnp.where(low_half, pltpu.roll(p, 64, 1), q)], 0
        )

    def done(slot):
        @pl.when(me > 0)
        def _():
            face_copy(slot).wait_send()
            pltpu.make_async_copy(rbuf.at[slot], rbuf.at[slot], frecv.at[slot]).wait()

        @pl.when(me < n - 1)
        def _():
            face_copy(slot + 1).wait_send()
            pltpu.make_async_copy(rbuf.at[slot + 1], rbuf.at[slot + 1], frecv.at[slot + 1]).wait()

    pack(
        jnp.concatenate(
            [
                plane_sum(
                    mask
                    * jnp.where(
                        low, fld[f * ne:(f + 1) * ne, 0:128].astype(F32), fld[f * ne:(f + 1) * ne, 384:512].astype(F32)
                    )
                )
                for f in range(nf)
            ],
            0,
        ),
        0,
    )

    l_lam.wait()
    for f in range(nf):
        rs = slice(f * ne, (f + 1) * ne)
        lw[rs] = -wts[0:1] * lam[rs].astype(F32)
    l_vel.wait()
    for d in range(3):
        for t in range(2):
            cols = slice(t * 256, t * 256 + 256)
            if d == 0:
                grad = jnp.dot(lam[...], fa[:, cols], preferred_element_type=F32)
            else:
                grad = jnp.dot(lam[:, cols], fbc[:, (d - 1) * 256:d * 256], preferred_element_type=F32)
            flow = vel[d * ne:(d + 1) * ne, cols].astype(F32)
            for f in range(nf):
                rs = slice(f * ne, (f + 1) * ne)
                flux = (lw[rs, cols] * flow - (diff[f] * wts[0:1, cols]) * grad[rs]).astype(BF16)
                if d == 0:
                    q0[rs, cols] = flux
                else:
                    qbc[t, rs, (d - 1) * 256:d * 256] = flux

    low_rows = lax.broadcasted_iota(jnp.int32, (rows, 128), 1) < 64
    q1f = jnp.where(low_rows, qbc[0, :, 0:128], qbc[1, :, 128:256])
    q2f = jnp.where(low_rows, qbc[0, :, 256:384], qbc[1, :, 384:512])
    face = jnp.dot(q0[...], bfa[...], preferred_element_type=F32) + jnp.dot(
        jnp.concatenate([q1f, q2f], 1), bfbc[...], preferred_element_type=F32
    )
    pack(jnp.concatenate([plane_sum(mask * face[f * ne:(f + 1) * ne]) for f in range(nf)], 0), 2)

    for t in range(2):
        cols = slice(t * 256, t * 256 + 256)
        back = jnp.dot(q0[...], ba[:, cols], preferred_element_type=F32) + jnp.dot(
            qbc[t], bbc[...], preferred_element_type=F32
        )
        for s in range(2):
            ct = slice(t * 256 + s * 128, t * 256 + s * 128 + 128)
            for f in range(nf):
                rs = slice(f * ne, (f + 1) * ne)
                base[rs, ct] = mask * plane_sum(mask * back[rs, s * 128:s * 128 + 128])
    for ct in range(4):
        cols = slice(ct * 128, ct * 128 + 128)
        mw = mask * wts[0:1, cols]
        u = [mw * plane_sum(mask * fld[f * ne:(f + 1) * ne, cols].astype(F32)) for f in range(nf)]
        for f in range(nf):
            rs = slice(f * ne, (f + 1) * ne)
            plain[rs, cols] = u[f]
            mixed[rs, cols] = sum(sym[f][h] * u[h] for h in range(nf))

    for o in range(1, n):
        copy = pltpu.make_async_remote_copy(
            src_ref=part, dst_ref=parts.at[o - 1], send_sem=psend.at[o - 1], recv_sem=precv.at[o - 1],
            device_id={"gx": lax.rem(me + o, n)}, device_id_type=pl.DeviceIdType.MESH,
        )
        copy.wait()
    total = part[...] + jnp.sum(parts[...], 0)
    trace = jnp.sum(total[0:8], keepdims=True)
    beta = jnp.sum(total[8:16], keepdims=True)
    c1 = jnp.broadcast_to(2.0 / trace, (1, 128))
    c2 = jnp.broadcast_to(-2.0 * beta / (trace * trace), (1, 128))
    for ct in (1, 2):
        cols = slice(ct * 128, ct * 128 + 128)
        out[:, cols] = base[:, cols] + c1 * mixed[:, cols] + c2 * plain[:, cols]

    done(0)
    got = unpack(0)
    wf = mask * jnp.where(low, wts[0:1, 0:128], wts[0:1, 384:512])
    u = [wf * got[f * ne:(f + 1) * ne] for f in range(nf)]
    extra = [c1 * sum(sym[f][h] * u[h] for h in range(nf)) + c2 * u[f] for f in range(nf)]
    for ct in (0, 3):
        cols = slice(ct * 128, ct * 128 + 128)
        for f in range(nf):
            rs = slice(f * ne, (f + 1) * ne)
            side = low if ct == 0 else ~low
            base[rs, cols] = (
                base[rs, cols] + c1 * mixed[rs, cols] + c2 * plain[rs, cols] + jnp.where(side, extra[f], 0.0)
            )
    done(2)
    got = unpack(2)
    for ct in (0, 3):
        cols = slice(ct * 128, ct * 128 + 128)
        for f in range(nf):
            rs = slice(f * ne, (f + 1) * ne)
            side = low if ct == 0 else ~low
            out[rs, cols] = base[rs, cols] + jnp.where(side, mask * got[rs], 0.0)


def per_device(n, fields, adjoint_seed, velocity, activity, diffusivity, gram_cotangent):
    nf, _, ne, nn = fields.shape
    rows = nf * ne
    table_shapes = ((nn, nn), (256, 512), (nn, nn), (512, 256), (nn, 128), (256, 128))
    vmem, anywhere = pl.BlockSpec(memory_space=pltpu.VMEM), pl.BlockSpec(memory_space=pltpu.HBM)
    smem = pl.BlockSpec(memory_space=pltpu.SMEM)
    result = pl.pallas_call(
        functools.partial(kernel, n, nf, ne),
        out_shape=pltpu.VMEM((rows, nn), F32),
        in_specs=[smem, smem, vmem] + [anywhere] * 4,
        out_specs=vmem,
        scratch_shapes=[
            pltpu.VMEM((rows, nn), BF16),
            pltpu.VMEM((rows, nn), BF16),
            pltpu.VMEM((3 * ne, nn), BF16),
            *[pltpu.VMEM(t, BF16) for t in table_shapes],
            pltpu.VMEM((8, 1536 + nn), F32),
            pltpu.VMEM((rows, nn), F32),
            pltpu.VMEM((rows, nn), BF16),
            pltpu.VMEM((2, rows, nn), BF16),
            pltpu.VMEM((rows, nn), F32),
            pltpu.VMEM((rows, nn), F32),
            pltpu.VMEM((rows, nn), F32),
            pltpu.VMEM((16, 128), F32),
            pltpu.VMEM((n - 1, 16, 128), F32),
            pltpu.VMEM((4, rows // 2, 128), F32),
            pltpu.VMEM((4, rows // 2, 128), F32),
            pltpu.SemaphoreType.DMA((4,)),
            pltpu.SemaphoreType.DMA((n - 1,)),
            pltpu.SemaphoreType.DMA((n - 1,)),
            pltpu.SemaphoreType.DMA((4,)),
            pltpu.SemaphoreType.DMA((4,)),
        ],
        compiler_params=pltpu.CompilerParams(
            collective_id=0, has_side_effects=True, vmem_limit_bytes=60 * 1024 * 1024
        ),
    )(
        diffusivity,
        gram_cotangent,
        activity,
        fields.reshape(rows, nn),
        adjoint_seed.reshape(rows, nn),
        velocity.reshape(3 * ne, nn),
        jnp.asarray(constants()),
    )
    return result.reshape(nf, 1, ne, nn)


def solution(mesh):
    spec = P(None, ("member", "gx"), None, None)
    return jax.shard_map(
        functools.partial(per_device, mesh.shape["gx"]),
        mesh=mesh,
        in_specs=(spec, spec, spec, P(("member", "gx"), None), P(), P()),
        out_specs=spec,
        check_vma=False,
    )
```

profile of v0, /device:TPU:1, one launch (start us, length us, event | category | flops | bytes accessed | tf_op | source)
XLA Modules:
  0.0 13.6 jit_solution(2609424600305729775)
XLA Ops:
  0.0 12.7 %shard_map.73 = f32[320,512]{1,0:T(8,128)S(1)} custom-call(f32[5]{0:T(128)} %diff.1, f32[5,5]{1,0:T(8,128)} %gram.1, s32[1,64]{1,0:T(1,128)} %act.1, bf16[320,512]{1,0:T(8,128)(2,1)} %bitcast.7, bf16[320,512]{1,0:T(8,128)(2,1)} %bitcast.8, bf16[192,512]{1,0:T(8,128)(2,1)} %bitcast.9, f32[8,2048]{1,0:T(8,128)} %constant.2.clone.spread_hbm), custom_call_target="tpu_custom_call" | custom-call | tf_op jit(solution)/shard_map/pallas_call | solution.py:335
  12.7 0.8 %copy.10 = f32[5,1,64,512]{3,2,1,0:T(8,128)} copy(f32[5,1,64,512]{3,2,1,0:T(8,128)S(1)} %bitcast.6) | data formatting | bytes 1310720
where the time goes:
time: 13.7 us; the launch traced here: 13.6 us
  Pallas kernels  12.7 us (93%)
  local copies, waits for them, and re-layouts  0.84 us (6%)
    pallas_call x1, Pallas kernels, per_device(): pl.pallas_call(functools.partial(kernel, n, nf, ne), out_shape=pltpu.VMEM...  12.7 us
    unnamed x1, local copies, waits for them, and re-layouts  0.84 us

commit v1 on v0

--- a/solution.py
+++ b/solution.py
@@ -100,7 +100,7 @@
     diff, gram, act, fld_hbm, lam_hbm, vel_hbm, spread_hbm,
     out,
     fld, lam, vel, fa, fbc, ba, bbc, bfa, bfbc, spread,
-    lw, q0, qbc, base, mixed, plain,
+    lw, q0, qbc, base, mixed, plain, ends,
     part, parts, sbuf, rbuf,
     in_sem, psend, precv, fsend, frecv,
 ):
@@ -174,8 +174,10 @@
         mw = mask * wts[0:1, cols]
         t_acc = t_acc + jnp.sum((mw * square).reshape(ne // 8, 8, 128), 0)
         b_acc = b_acc + jnp.sum((mw * quad).reshape(ne // 8, 8, 128), 0)
-    part[0:8] = t_acc
-    part[8:16] = b_acc
+    t_row = jnp.sum(t_acc, 0, keepdims=True)
+    b_row = jnp.sum(b_acc, 0, keepdims=True)
+    left = lax.broadcasted_iota(jnp.int32, (1, 128), 1) < 64
+    part[...] = jnp.where(left, t_row, b_row) + pltpu.roll(jnp.where(left, b_row, t_row), 64, 1)
 
     pl.semaphore_wait(barrier, n - 1)
 
@@ -288,42 +290,46 @@
             plain[rs, cols] = u[f]
             mixed[rs, cols] = sum(sym[f][h] * u[h] for h in range(nf))
 
+    done(0)
+    got = unpack(0)
+    wf = mask * jnp.where(low, wts[0:1, 0:128], wts[0:1, 384:512])
+    u = [wf * got[f * ne:(f + 1) * ne] for f in range(nf)]
+    for f in range(nf):
+        rs = slice(f * ne, (f + 1) * ne)
+        ends[0, rs] = u[f]
+        ends[1, rs] = sum(sym[f][h] * u[h] for h in range(nf))
+
     for o in range(1, n):
         copy = pltpu.make_async_remote_copy(
             src_ref=part, dst_ref=parts.at[o - 1], send_sem=psend.at[o - 1], recv_sem=precv.at[o - 1],
             device_id={"gx": lax.rem(me + o, n)}, device_id_type=pl.DeviceIdType.MESH,
         )
         copy.wait()
-    total = part[...] + jnp.sum(parts[...], 0)
-    trace = jnp.sum(total[0:8], keepdims=True)
-    beta = jnp.sum(total[8:16], keepdims=True)
+    total = part[...]
+    for o in range(1, n):
+        total = total + parts[o - 1]
+    trace = jnp.sum(jnp.where(left, total, 0.0), keepdims=True)
+    beta = jnp.sum(jnp.where(left, 0.0, total), keepdims=True)
     c1 = jnp.broadcast_to(2.0 / trace, (1, 128))
     c2 = jnp.broadcast_to(-2.0 * beta / (trace * trace), (1, 128))
-    for ct in (1, 2):
-        cols = slice(ct * 128, ct * 128 + 128)
-        out[:, cols] = base[:, cols] + c1 * mixed[:, cols] + c2 * plain[:, cols]
-
-    done(0)
-    got = unpack(0)
-    wf = mask * jnp.where(low, wts[0:1, 0:128], wts[0:1, 384:512])
-    u = [wf * got[f * ne:(f + 1) * ne] for f in range(nf)]
-    extra = [c1 * sum(sym[f][h] * u[h] for h in range(nf)) + c2 * u[f] for f in range(nf)]
-    for ct in (0, 3):
-        cols = slice(ct * 128, ct * 128 + 128)
-        for f in range(nf):
-            rs = slice(f * ne, (f + 1) * ne)
-            side = low if ct == 0 else ~low
-            base[rs, cols] = (
-                base[rs, cols] + c1 * mixed[rs, cols] + c2 * plain[rs, cols] + jnp.where(side, extra[f], 0.0)
-            )
+    for f in range(nf):
+        rs = slice(f * ne, (f + 1) * ne)
+        end = c1 * ends[1, rs] + c2 * ends[0, rs]
+        for ct in range(4):
+            cols = slice(ct * 128, ct * 128 + 128)
+            value = base[rs, cols] + c1 * mixed[rs, cols] + c2 * plain[rs, cols]
+            if ct == 0:
+                value = value + jnp.where(low, end, 0.0)
+            if ct == 3:
+                value = value + jnp.where(low, 0.0, end)
+            out[rs, cols] = value
     done(2)
     got = unpack(2)
-    for ct in (0, 3):
-        cols = slice(ct * 128, ct * 128 + 128)
-        for f in range(nf):
-            rs = slice(f * ne, (f + 1) * ne)
-            side = low if ct == 0 else ~low
-            out[rs, cols] = base[rs, cols] + jnp.where(side, mask * got[rs], 0.0)
+    for f in range(nf):
+        rs = slice(f * ne, (f + 1) * ne)
+        end = mask * got[rs]
+        out[rs, 0:128] = out[rs, 0:128] + jnp.where(low, end, 0.0)
+        out[rs, 384:512] = out[rs, 384:512] + jnp.where(low, 0.0, end)
 
 
 def per_device(n, fields, adjoint_seed, velocity, activity, diffusivity, gram_cotangent):
@@ -349,8 +355,9 @@
             pltpu.VMEM((rows, nn), F32),
             pltpu.VMEM((rows, nn), F32),
             pltpu.VMEM((rows, nn), F32),
-            pltpu.VMEM((16, 128), F32),
-            pltpu.VMEM((n - 1, 16, 128), F32),
+            pltpu.VMEM((2, rows, 128), F32),
+            pltpu.VMEM((1, 128), F32),
+            pltpu.VMEM((n - 1, 1, 128), F32),
             pltpu.VMEM((4, rows // 2, 128), F32),
             pltpu.VMEM((4, rows // 2, 128), F32),
             pltpu.SemaphoreType.DMA((4,)),

time: 13.7 us -> 12.5 us (0.912)
  Pallas kernels: 12.7 us -> 11.5 us
    pallas_call x1, Pallas kernels: 12.7 us -> 11.5 us  [per_device(): pl.pallas_call(functools.partial(kernel, n, nf, ne), out_shape=pltpu.VMEM...]
where the time goes in v1:
time: 12.5 us; the launch traced here: 12.4 us
  Pallas kernels  11.5 us (92%)
  local copies, waits for them, and re-layouts  0.84 us (7%)
    pallas_call x1, Pallas kernels, per_device(): pl.pallas_call(functools.partial(kernel, n, nf, ne), out_shape=pltpu.VMEM...  11.5 us
    unnamed x1, local copies, waits for them, and re-layouts  0.84 us

profile of v1, /device:TPU:1, one launch (start us, length us, event | category | flops | bytes accessed | tf_op | source)
XLA Modules:
  0.0 12.4 jit_solution(10538138992787772906)
XLA Ops:
  0.0 11.5 %shard_map.73 = f32[320,512]{1,0:T(8,128)S(1)} custom-call(f32[5]{0:T(128)} %diff.1, f32[5,5]{1,0:T(8,128)} %gram.1, s32[1,64]{1,0:T(1,128)} %act.1, bf16[320,512]{1,0:T(8,128)(2,1)} %bitcast.7, bf16[320,512]{1,0:T(8,128)(2,1)} %bitcast.8, bf16[192,512]{1,0:T(8,128)(2,1)} %bitcast.9, f32[8,2048]{1,0:T(8,128)} %constant.2.clone.spread_hbm), custom_call_target="tpu_custom_call" | custom-call | tf_op jit(solution)/shard_map/pallas_call | solution.py:341
  11.5 0.8 %copy.10 = f32[5,1,64,512]{3,2,1,0:T(8,128)} copy(f32[5,1,64,512]{3,2,1,0:T(8,128)S(1)} %bitcast.6) | data formatting | bytes 1310720

commit v2 on v1

--- a/solution.py
+++ b/solution.py
@@ -97,9 +97,9 @@
 
 def kernel(
     n, nf, ne,
-    diff, gram, act, fld_hbm, lam_hbm, vel_hbm, spread_hbm,
+    diff_hbm, gram_hbm, act_hbm, fld_hbm, lam_hbm, vel_hbm, spread_hbm,
     out,
-    fld, lam, vel, fa, fbc, ba, bbc, bfa, bfbc, spread,
+    fld, lam, vel, fa, fbc, ba, bbc, bfa, bfbc, spread, diff, gram, act,
     lw, q0, qbc, base, mixed, plain, ends,
     part, parts, sbuf, rbuf,
     in_sem, psend, precv, fsend, frecv,
@@ -108,11 +108,13 @@
     rows = nf * ne
     half = rows // 2
 
-    pairs = ((spread_hbm, spread), (fld_hbm, fld), (lam_hbm, lam), (vel_hbm, vel))
+    pairs = (
+        (act_hbm, act), (gram_hbm, gram), (diff_hbm, diff), (spread_hbm, spread), (fld_hbm, fld), (lam_hbm, lam), (vel_hbm, vel),
+    )
     loads = [pltpu.make_async_copy(s, d, in_sem.at[i]) for i, (s, d) in enumerate(pairs)]
     for load in loads:
         load.start()
-    l_spread, l_fld, l_lam, l_vel = loads
+    l_act, l_gram, l_diff, l_spread, l_fld, l_lam, l_vel = loads
 
     barrier = pltpu.get_barrier_semaphore()
 
@@ -148,6 +150,9 @@
         down = jnp.concatenate([x[ne - EZ:], x[: ne - EZ]], 0)
         return x + jnp.where(y_hi, pltpu.roll(up, 56, 1), 0.0) + jnp.where(y_lo, pltpu.roll(down, 72, 1), 0.0)
 
+    l_act.wait()
+    l_gram.wait()
+    l_diff.wait()
     flag_row = jnp.broadcast_to(act[...].astype(F32), (ne, ne))
     diag = lax.broadcasted_iota(jnp.int32, (ne, ne), 0) == lax.broadcasted_iota(jnp.int32, (ne, ne), 1)
     mask = jnp.dot(
@@ -337,11 +342,10 @@
     rows = nf * ne
     table_shapes = ((nn, nn), (256, 512), (nn, nn), (512, 256), (nn, 128), (256, 128))
     vmem, anywhere = pl.BlockSpec(memory_space=pltpu.VMEM), pl.BlockSpec(memory_space=pltpu.HBM)
-    smem = pl.BlockSpec(memory_space=pltpu.SMEM)
     result = pl.pallas_call(
         functools.partial(kernel, n, nf, ne),
         out_shape=pltpu.VMEM((rows, nn), F32),
-        in_specs=[smem, smem, vmem] + [anywhere] * 4,
+        in_specs=[anywhere] * 7,
         out_specs=vmem,
         scratch_shapes=[
             pltpu.VMEM((rows, nn), BF16),
@@ -349,6 +353,9 @@
             pltpu.VMEM((3 * ne, nn), BF16),
             *[pltpu.VMEM(t, BF16) for t in table_shapes],
             pltpu.VMEM((8, 1536 + nn), F32),
+            pltpu.SMEM(diffusivity.shape, F32),
+            pltpu.SMEM(gram_cotangent.shape, F32),
+            pltpu.VMEM(activity.shape, jnp.int32),
             pltpu.VMEM((rows, nn), F32),
             pltpu.VMEM((rows, nn), BF16),
             pltpu.VMEM((2, rows, nn), BF16),
@@ -360,7 +367,7 @@
             pltpu.VMEM((n - 1, 1, 128), F32),
             pltpu.VMEM((4, rows // 2, 128), F32),
             pltpu.VMEM((4, rows // 2, 128), F32),
-            pltpu.SemaphoreType.DMA((4,)),
+            pltpu.SemaphoreType.DMA((7,)),
             pltpu.SemaphoreType.DMA((n - 1,)),
             pltpu.SemaphoreType.DMA((n - 1,)),
             pltpu.SemaphoreType.DMA((4,)),

time: 12.5 us -> 11.8 us (0.944)
  Pallas kernels: 11.5 us -> 10.8 us
    pallas_call x1, Pallas kernels: 11.5 us -> 10.8 us  [per_device(): pl.pallas_call(functools.partial(kernel, n, nf, ne), out_shape=pltpu.VMEM...]
where the time goes in v2:
time: 11.8 us; the launch traced here: 11.6 us
  Pallas kernels  10.8 us (92%)
  local copies, waits for them, and re-layouts  0.84 us (7%)
    pallas_call x1, Pallas kernels, per_device(): pl.pallas_call(functools.partial(kernel, n, nf, ne), out_shape=pltpu.VMEM...  10.8 us
    unnamed x1, local copies, waits for them, and re-layouts  0.84 us

profile of v2, /device:TPU:1, one launch (start us, length us, event | category | flops | bytes accessed | tf_op | source)
XLA Modules:
  0.0 11.6 jit_solution(7715116311749964944)
XLA Ops:
  0.0 10.8 %shard_map.73 = f32[320,512]{1,0:T(8,128)S(1)} custom-call(f32[5]{0:T(128)} %diff_hbm.1, f32[5,5]{1,0:T(8,128)} %gram_hbm.1, s32[1,64]{1,0:T(1,128)} %act_hbm.1, bf16[320,512]{1,0:T(8,128)(2,1)} %bitcast.7, bf16[320,512]{1,0:T(8,128)(2,1)} %bitcast.8, bf16[192,512]{1,0:T(8,128)(2,1)} %bitcast.9, f32[8,2048]{1,0:T(8,128)} %constant.2.clone.spread_hbm), custom_call_target="tpu_custom_call" | custom-call | tf_op jit(solution)/shard_map/pallas_call | solution.py:345
  10.8 0.8 %copy.10 = f32[5,1,64,512]{3,2,1,0:T(8,128)} copy(f32[5,1,64,512]{3,2,1,0:T(8,128)S(1)} %bitcast.6) | data formatting | bytes 1310720
